TPU v7x, 512 devices: a whole 4x4x16 slice. The times are simulated.
512 devices in a mesh: space: 128 (over z, y, core), code: 4 (over x).
Axes of the slice: x: 4, y: 4, z: 16, core: 2. Of those that a mesh axis runs over, the one named last changes fastest.
Arguments:
- geometry: bfloat16 [4, 6, 1048576], P('code', None, 'space'), as said below
- codebook: bfloat16 [48, 4096], P(None, 'code'), may hold values from -3 to 3
- word_ids: int32 [1048576], P('space'), may hold values from 0 to 4095
- residual: bfloat16 [12, 1048576], P(None, 'space'), may hold values from -2 to 2
- send_list: int32 [4, 128, 128], P('code', 'space'), may hold values from 0 to 63
- tile_list: int32 [4, 1024, 4], P('code', 'space'), may hold values from 0 to 127, as said below
- rays: float32 [4, 3, 262144], P('code', None, 'space'), as said below
- target: int32 [4, 3, 262144], P('code', None, 'space'), may hold values from 0 to 255
Outputs:
- rendered: float32 [4, 3, 262144], P('code', None, 'space')
- foot_grad: float32 [4, 6, 1048576], P('code', None, 'space')
- resid_grad: float32 [12, 1048576], P(None, 'space')
- code_grad: float32 [48, 4096], P(None, 'code')
Inputs may be any that keep to these rules, and one draw needn't show every extreme that they name: `tile_list`: each row names 4 different owners. `geometry`: conics are positive definite, |b| at most 0.6 sqrt(a c); opacities are positive and at most 0.5. `rays`: every ray has length 0.8 to 1.2; directions may point anywhere.
All inputs are finite; a program needn't handle non-finite values.
Results may differ from a plain program's by a relative error of at most 0.0021.
Values may be sent and summed in bfloat16 or wider, within the bound.
A program may use at most 64 MiB of HBM per device.

v0:
```python
import math
import jax
import jax.numpy as jnp
from jax import lax
from jax.sharding import PartitionSpec as P

WORDS = 4096
COEF = 48
RESID = 12
GEO = 6
BLOCK = 128
LIST = 4
SIDE = 16
TILE_PIX = 256
band_zero = 0.28209479177387814
band_one = 0.4886025119029199
band_two = (
    1.0925484305920792,
    -1.0925484305920792,
    0.31539156525252005,
    -1.0925484305920792,
    0.5462742152960396,
)
band_three = (
    -0.5900435899266435,
    2.890611442640554,
    -0.4570457994644658,
    0.3731763325901154,
    -0.4570457994644658,
    1.445305721320277,
    -0.5900435899266435,
)


def harmonics(direction):
    length = jnp.sqrt(jnp.sum(direction * direction, axis=0))
    coord_x = direction[0] / length
    coord_y = direction[1] / length
    coord_z = direction[2] / length
    square_x = coord_x * coord_x
    square_y = coord_y * coord_y
    square_z = coord_z * coord_z
    entries = [
        band_zero * jnp.ones_like(coord_x),
        -band_one * coord_y,
        band_one * coord_z,
        -band_one * coord_x,
        band_two[0] * coord_x * coord_y,
        band_two[1] * coord_y * coord_z,
        band_two[2] * (2.0 * square_z - square_x - square_y),
        band_two[3] * coord_x * coord_z,
        band_two[4] * (square_x - square_y),
        band_three[0] * coord_y * (3.0 * square_x - square_y),
        band_three[1] * coord_x * coord_y * coord_z,
        band_three[2] * coord_y * (4.0 * square_z - square_x - square_y),
        band_three[3] * coord_z * (2.0 * square_z - 3.0 * square_x - 3.0 * square_y),
        band_three[4] * coord_x * (4.0 * square_z - square_x - square_y),
        band_three[5] * coord_z * (square_x - square_y),
        band_three[6] * coord_x * (square_x - 3.0 * square_y),
    ]
    return jnp.stack(entries)


def pixel_offsets(side):
    pixel_index = jnp.arange(side * side, dtype=jnp.int32)
    offset_u = (pixel_index % side).astype(jnp.float32) - (side - 1) * 0.5
    offset_v = (pixel_index // side).astype(jnp.float32) - (side - 1) * 0.5
    return jnp.stack([offset_u, offset_v])


def composite(footprint, palette, harmonic_rows, offsets):
    delta_u = offsets[0][:, None] - footprint[0][None, :]
    delta_v = offsets[1][:, None] - footprint[1][None, :]
    exponent = -0.5 * (
        footprint[2] * delta_u * delta_u
        + 2.0 * footprint[3] * delta_u * delta_v
        + footprint[4] * delta_v * delta_v
    )
    absorb = footprint[5] * jnp.exp(exponent)
    keep_log = jnp.log1p(-absorb)
    before = jnp.cumsum(keep_log, axis=1) - keep_log
    weight = jnp.exp(before) * absorb
    mixed = jnp.dot(weight, palette.T, precision=lax.Precision.HIGHEST)
    mixed = mixed.reshape(mixed.shape[0], 16, 3)
    return (
        jnp.einsum("kp,pkc->cp", harmonic_rows, mixed, precision=lax.Precision.HIGHEST)
        + 0.5 * jnp.sum(weight, axis=1)[None, :]
    )


def render_group(footprint, palette, harmonic_rows, destination_group, offsets):

    def forward(foot_all, palette_group):
        return jax.vmap(composite, in_axes=(0, 0, 0, None))(
            foot_all, palette_group, harmonic_rows, offsets
        )

    images, pullback = jax.vjp(forward, footprint, palette)
    grad_foot, grad_palette = pullback(images - destination_group)
    return (images, grad_foot, grad_palette)


def decode(codebook, word_ids, residual):
    looked = jnp.take(codebook, word_ids, axis=1).astype(jnp.float32)
    upper = looked[:RESID] + residual.astype(jnp.float32)
    decoded = jnp.concatenate([upper, looked[RESID:]], axis=0).astype(jnp.bfloat16)
    return lax.optimization_barrier(decoded)


def on_device(geometry, codebook, word_ids, residual, send_list, tile_list, rays, target):
    n_space = lax.axis_size("space")
    blocks = word_ids.shape[0] // BLOCK
    tiles_here = tile_list.shape[1]
    list_width = LIST * BLOCK
    full_book = lax.all_gather(codebook, "code", axis=1, tiled=True)
    sent_blocks = send_list[0, 0]
    foot_out = jnp.take(geometry[0].reshape(GEO, blocks, BLOCK), sent_blocks, axis=1)
    decoded = decode(full_book, word_ids, residual)
    palette_out = jnp.take(decoded.reshape(COEF, blocks, BLOCK), sent_blocks, axis=1)
    foot_in, palette_in = (
        lax.all_to_all(foot_out, "space", split_axis=1, concat_axis=1, tiled=True),
        lax.all_to_all(palette_out, "space", split_axis=1, concat_axis=1, tiled=True),
    )
    tile_rows = tile_list[0]
    flat_rows = tile_rows.reshape(-1)
    foot_tiles = (
        jnp.take(foot_in, flat_rows, axis=1).reshape(GEO, tiles_here, list_width).transpose(1, 0, 2)
    )
    palette_tiles = (
        jnp.take(palette_in, flat_rows, axis=1)
        .reshape(COEF, tiles_here, list_width)
        .transpose(1, 0, 2)
    )
    harmonic_tiles = harmonics(rays[0]).reshape(16, tiles_here, TILE_PIX).transpose(1, 0, 2)
    target_tiles = (
        (target[0].astype(jnp.float32) / 255.0).reshape(3, tiles_here, TILE_PIX).transpose(1, 0, 2)
    )
    per_step = math.gcd(tiles_here, 2)
    step_count = tiles_here // per_step
    offsets = pixel_offsets(SIDE)

    def render_step(inputs):
        foot_group, palette_group, harmonic_group, destination_group = inputs
        return render_group(
            foot_group.astype(jnp.float32),
            palette_group.astype(jnp.float32),
            harmonic_group,
            destination_group,
            offsets,
        )

    images, grad_foot, grad_palette = lax.map(
        render_step,
        (
            foot_tiles.reshape(step_count, per_step, GEO, list_width),
            palette_tiles.reshape(step_count, per_step, COEF, list_width),
            harmonic_tiles.reshape(step_count, per_step, 16, TILE_PIX),
            target_tiles.reshape(step_count, per_step, 3, TILE_PIX),
        ),
    )
    tile_grads = jnp.concatenate(
        [
            grad_foot.reshape(tiles_here, GEO, list_width),
            grad_palette.reshape(tiles_here, COEF, list_width),
        ],
        axis=1,
    )
    tile_grads = tile_grads.reshape(tiles_here, GEO + COEF, LIST, BLOCK)
    slot_hot = (
        tile_rows[:, :, None] == jnp.arange(n_space, dtype=jnp.int32)[None, None, :]
    ).astype(jnp.float32)
    slot_grads = jnp.einsum("tln,tclk->cnk", slot_hot, tile_grads, precision=lax.Precision.HIGHEST)
    sent_hot = (sent_blocks[:, None] == jnp.arange(blocks, dtype=jnp.int32)[None, :]).astype(
        jnp.float32
    )
    returned = lax.all_to_all(slot_grads, "space", split_axis=1, concat_axis=1, tiled=True)
    owned = jnp.einsum("cnk,nb->cbk", returned, sent_hot, precision=lax.Precision.HIGHEST).reshape(
        GEO + COEF, blocks * BLOCK
    )
    palette_owned = owned[GEO:]
    word_term = jax.ops.segment_sum(palette_owned.T, word_ids, num_segments=WORDS).T
    resid_part = palette_owned[:RESID]
    foot_grad = owned[:GEO]
    resid_grad = lax.psum(resid_part, "code")
    codeword_portion = lax.psum_scatter(word_term, "code", scatter_dimension=1, tiled=True)
    code_grad = lax.psum(codeword_portion, "space")
    rendered = (
        images.reshape(tiles_here, 3, TILE_PIX)
        .transpose(1, 0, 2)
        .reshape(1, 3, tiles_here * TILE_PIX)
    )
    return (rendered, foot_grad[None], resid_grad, code_grad)


def solution(mesh):
    placed = (
        P("code", None, "space"),
        P(None, "code"),
        P("space"),
        P(None, "space"),
        P("code", "space", None),
        P("code", "space", None),
        P("code", None, "space"),
        P("code", None, "space"),
    )
    return jax.shard_map(
        on_device,
        mesh=mesh,
        in_specs=placed,
        out_specs=(
            P("code", None, "space"),
            P("code", None, "space"),
            P(None, "space"),
            P(None, "code"),
        ),
        check_vma=False,
    )
```

profile of v0, /device:TPU:8, one launch (start us, length us, event | category | flops | bytes accessed | tf_op | source)
XLA Modules:
  0.0 950.6 jit_solution(1836377726024788179)
XLA Ops:
  7.2 0.7 compare_and_fusion.1
  8.5 0.7 gather_fusion
  9.2 0.9 select_bitcast_fusion.3
  10.2 19.5 %all-to-all-start = ((bf16[6,128,128]{2,0,1:T(8,128)(2,1)}), bf16[6,128,128]{2,0,1:T(8,128)(2,1)S(1)}, u32[]{:S(2)}, u32[]{:S(2)}) async-start(bf16[6,128,128]{2,0,1:T(8,128)(2,1)} %select_bitcast_fusion.3), calls=%async_computation | async-start | bytes 524288 | tf_op jit(solution)/shard_map/all_to_all | solution.py:121
  29.7 0.8 compare_and_fusion
  30.4 1.4 fusion.63
  31.8 1.1 copy.230
  32.9 14.9 %all_gather.3 = bf16[48,4096]{0,1:T(8,128)(2,1)S(1)} all-gather(bf16[48,1024]{0,1:T(8,128)(2,1)S(1)} %copy.230), channel_id=1, replica_groups=mesh['space'=128,'code'=4] {'code'}, dimensions={1}, use_global_device_ids=true | all-gather | bytes 491520 | tf_op jit(solution)/shard_map/all_gather | solution.py:115
  47.8 27.9 %gather_fusion.2 = bf16[8192,48]{1,0:T(8,128)(2,1)S(1)} fusion(bf16[48,4096]{0,1:T(8,128)(2,1)S(1)} %all_gather.3, s32[8192]{0:T(1024)} %fusion.63), kind=kCustom, calls=%fused_computation.2 | custom fusion | bytes 1605632 | tf_op jit(solution)/shard_map/jit(_take)/gather | solution.py:104
  75.7 0.8 copy.231
  77.9 0.9 gather_fusion.3
  78.8 1.4 select_bitcast_fusion
  80.2 16.2 %all-to-all-start.1 = ((bf16[48,128,128]{2,0,1:T(8,128)(2,1)}), bf16[48,128,128]{2,0,1:T(8,128)(2,1)S(1)}, u32[]{:S(2)}, u32[]{:S(2)}) async-start(bf16[48,128,128]{2,0,1:T(8,128)(2,1)} %select_bitcast_fusion), calls=%async_computation.1 | async-start | bytes 3145728 | tf_op jit(solution)/shard_map/all_to_all | solution.py:122
  98.1 1.5 gather_fusion.1
  99.7 71.7 %all-to-all-done.1 = bf16[48,128,128]{2,0,1:T(8,128)(2,1)S(1)} async-done(((bf16[48,128,128]{2,0,1:T(8,128)(2,1)}), bf16[48,128,128]{2,0,1:T(8,128)(2,1)S(1)}, u32[]{:S(2)}, u32[]{:S(2)}) %all-to-all-start.1) | async-done | bytes 1572896 | tf_op jit(solution)/shard_map/all_to_all | solution.py:122
  172.5 0.9 copy.256
  173.4 107.2 %while.16 = (s32[]{:T(128)}, f32[4,2,3,256]{3,1,0,2:T(2,128)S(1)}, f32[4,2,6,512]{3,2,1,0:T(8,128)}, f32[4,2,48,512]{3,2,1,0:T(8,128)}, bf16[4,2,6,512]{3,1,0,2:...) while((s32[]{:T(128)}, f32[4,2,3,256]{3,1,0,2:T(2,128)S(1)}, ...), condition=%wide.region_14.15_spmd.clone.clone, body=%wide.region_1.14_spmd.clone.clone.sunk | while | flops 552732160 | bytes 30296212 | solution.py:152
  174.4 1.9 fusion.93
  176.4 2.6 multiply_reduce_fusion.7
  180.0 2.6 fusion.94
  182.7 0.7 fusion.95
  183.5 2.4 fusion.98
  185.9 3.5 multiply_multiply_fusion.3
  190.4 4.3 fusion.96
  195.9 3.5 fusion.97
  201.2 1.9 fusion.93
  203.2 2.6 multiply_reduce_fusion.7
  206.8 2.6 fusion.94
  209.5 0.7 fusion.95
  210.3 2.4 fusion.98
  212.7 3.5 multiply_multiply_fusion.3
  217.1 4.3 fusion.96
  222.7 3.5 fusion.97
  228.0 1.9 fusion.93
  229.9 2.6 multiply_reduce_fusion.7
  233.6 2.6 fusion.94
  236.3 0.7 fusion.95
  237.0 2.4 fusion.98
  239.5 3.5 multiply_multiply_fusion.3
  243.9 4.3 fusion.96
  249.5 3.5 fusion.97
  254.8 1.9 fusion.93
  256.7 2.6 multiply_reduce_fusion.7
  260.3 2.6 fusion.94
  263.1 0.7 fusion.95
  263.8 2.5 fusion.98
  266.3 3.5 multiply_multiply_fusion.3
  270.7 4.3 fusion.96
  276.3 3.5 fusion.97
  280.5 1.4 concatenate.15
  281.9 0.9 reshape.770
  282.9 4.8 convolution_bitcast_fusion.1
  287.6 4.5 copy.243
  292.1 171.6 %all_to_all.15 = f32[54,128,128]{2,0,1:T(8,128)S(1)} all-to-all(f32[54,128,128]{2,0,1:T(8,128)} %copy.243), channel_id=1, replica_groups=mesh['space'=128,'code'=4] {'space'}, dimensions={1} | all-to-all | bytes 7077888 | tf_op jit(solution)/shard_map/all_to_all | solution.py:176
  463.8 1.7 fusion.53
  465.7 2.7 copy.258
  468.4 45.7 %scatter_custom_fusion = f32[4096,48]{1,0:T(8,128)} fusion(s32[8192]{0:T(1024)} %param.12, f32[8192,48]{1,0:T(8,128)} %bitcast.185, f32[]{:T(128)} %constant.114.clone.1), kind=kCustom, calls=%fused_computation.109 | custom fusion | flops 393216 | bytes 786944 | tf_op jit(solution)/shard_map/scatter-add | solution.py:181
  514.1 35.1 %reduce-scatter.2.cloned.1.call-done = f32[48,1024]{0,1:T(8,128)} async-done(((f32[48,4096]{0,1:T(8,128)}), f32[48,1024]{0,1:T(8,128)}) %reduce-scatter.2.cloned.1.call-update) | async-done | bytes 196624 | tf_op jit(solution)/shard_map/reduce_scatter | solution.py:185
  549.4 1.1 copy.268
  551.2 0.7 slice.122
  551.9 332.1 %all-reduce.11.cloned.1.call-done = f32[48,1024]{0,1:T(8,128)} async-done(((f32[48,1024]{0,1:T(8,128)}), f32[48,1024]{0,1:T(8,128)}) %all-reduce.11.cloned.1.call-update) | async-done | bytes 196624 | tf_op jit(solution)/shard_map/psum | solution.py:186
  884.0 1.9 copy.248
  885.9 56.3 %all-reduce.9.cloned.1.call-done = f32[12,8192]{1,0:T(8,128)} async-done(((f32[12,8192]{1,0:T(8,128)}), f32[12,8192]{1,0:T(8,128)}) %all-reduce.9.cloned.1.call-update) | async-done | bytes 393232 | tf_op jit(solution)/shard_map/psum | solution.py:184
  942.2 1.9 copy.344
  (265 shorter events, 25.9 us)
Async XLA Ops:
  7.2 1.4 copy-start
  10.2 70.0 %all-to-all-start = ((bf16[6,128,128]{2,0,1:T(8,128)(2,1)}), bf16[6,128,128]{2,0,1:T(8,128)(2,1)S(1)}, u32[]{:S(2)}, u32[]{:S(2)}) async-start(bf16[6,128,128]{2,0,1:T(8,128)(2,1)} %select_bitcast_fusion.3), calls=%async_computation | async-start | bytes 524288 | tf_op jit(solution)/shard_map/all_to_all | solution.py:121
  76.6 1.0 copy-start.2
  80.2 16.4 %copy-start.6 = (s32[1,8,4]{1,2,0:T(4,128)S(1)}, s32[1,8,4]{1,2,0:T(4,128)}, u32[]{:S(2)}) copy-start(s32[1,8,4]{1,2,0:T(4,128)} %param.15) | copy-start | bytes 388
  80.2 16.6 %copy-start.3 = (f32[1,3,2048]{2,0,1:T(1,128)S(1)}, f32[1,3,2048]{2,0,1:T(1,128)}, u32[]{:S(2)}) copy-start(f32[1,3,2048]{2,0,1:T(1,128)} %param.16) | copy-start | bytes 73732
  80.2 16.8 %copy-start.4 = (s32[1,3,2048]{2,0,1:T(1,128)S(1)}, s32[1,3,2048]{2,0,1:T(1,128)}, u32[]{:S(2)}) copy-start(s32[1,3,2048]{2,0,1:T(1,128)} %param.17) | copy-start | bytes 73732
  80.2 17.7 %copy-start.1 = (bf16[6,128,128]{2,0,1:T(8,128)(2,1)}, bf16[6,128,128]{2,0,1:T(8,128)(2,1)S(1)}, u32[]{:S(2)}) copy-start(bf16[6,128,128]{2,0,1:T(8,128)(2,1)S(1)} %all-to-all-done) | copy-start | bytes 589828
  80.2 91.3 %all-to-all-start.1 = ((bf16[48,128,128]{2,0,1:T(8,128)(2,1)}), bf16[48,128,128]{2,0,1:T(8,128)(2,1)S(1)}, u32[]{:S(2)}, u32[]{:S(2)}) async-start(bf16[48,128,128]{2,0,1:T(8,128)(2,1)} %select_bitcast_fusion), calls=%async_computation.1 | async-start | bytes 3145728 | tf_op jit(solution)/shard_map/all_to_all | solution.py:122
  96.4 452.8 %reduce-scatter.2.cloned.1.call-start = ((), (), s32[]{:S(2)}) async-start(), calls=%async_computation.5 | async-start | bytes 2621440 | tf_op jit(solution)/shard_map/reduce_scatter | solution.py:185
  99.6 73.7 %copy-start.5 = (f32[4,2,3,256]{3,1,0,2:T(2,128)S(1)}, f32[4,2,3,256]{3,1,0,2:T(2,128)}, u32[]{:S(2)}) copy-start(f32[4,2,3,256]{3,1,0,2:T(2,128)} %custom-call.11) | copy-start | bytes 73732
  292.1 171.7 %copy-start.7 = (s32[1,1,128]{2,1,0:T(1,128)S(1)}, s32[1,1,128]{2,1,0:T(1,128)}, u32[]{:S(2)}) copy-start(s32[1,1,128]{2,1,0:T(1,128)} %param.14) | copy-start | bytes 1540
  514.1 369.9 %all-reduce.11.cloned.1.call-start = ((), (), s32[]{:S(2)}) async-start(), calls=%async_computation.6 | async-start | bytes 1048576 | tf_op jit(solution)/shard_map/psum | solution.py:186
  549.3 392.9 %all-reduce.9.cloned.1.call-start = ((), (), s32[]{:S(2)}) async-start(), calls=%async_computation.4 | async-start | bytes 1048576 | tf_op jit(solution)/shard_map/psum | solution.py:184
Sparse Core Ops, SparseCore 0:
  514.2 34.9 reduce-scatter.1
  553.1 330.8 all-reduce.10
  886.9 55.2 all-reduce.8
where the time goes:
time: 952 us; the launch traced here: 951 us
  waiting for transfers between devices  495 us (52%)
  blocking collectives  187 us (20%)
  other arithmetic  108 us (11%)
  local copies, waits for them, and re-layouts  69 us (7%)
  matrix products  40.4 us (4%)
  starting transfers between devices  35.9 us (4%)
  between operations  14.2 us (1%)
    psum x1, waiting for transfers between devices, on_device(): code_grad = lax.psum(codeword_portion, 'space')  332 us
    all_to_all x1, blocking collectives, on_device(): lax.all_to_all(slot_grads, 'space', split_axis=1, concat_axis=1, tiled=True)  172 us
    all_to_all x1, waiting for transfers between devices, on_device(): lax.all_to_all(palette_out, 'space', split_axis=1, concat_axis=1, tiled=T...  71.7 us
    psum x1, waiting for transfers between devices, on_device(): resid_grad = lax.psum(resid_part, 'code')  56.3 us
    scatter-add x1, other arithmetic, on_device(): jax.ops.segment_sum(palette_owned.T, word_ids, num_segments=WORDS)  45.7 us
    reduce_scatter x1, waiting for transfers between devices, on_device(): lax.psum_scatter(word_term, 'code', scatter_dimension=1, tiled=True)  35.1 us
    dot_general x12, matrix products, composite(): mixed = jnp.dot(weight, palette.T, precision=lax.Precision.HIGHEST)  33.9 us
    gather x2, local copies, waits for them, and re-layouts, decode(): looked = jnp.take(codebook, word_ids, axis=1).astype(jnp.float32)  28.8 us
  transfers between devices with their start and end apart: 5, of which 4 were waited for; matrix products, arithmetic and copies ran while one was open for 4% of the time, Pallas kernels for 0%

commit v1 on v0

--- a/solution.py
+++ b/solution.py
@@ -183,7 +183,7 @@
     foot_grad = owned[:GEO]
     resid_grad = lax.psum(resid_part, "code")
     codeword_portion = lax.psum_scatter(word_term, "code", scatter_dimension=1, tiled=True)
-    code_grad = lax.psum(codeword_portion, "space")
+    code_grad = jnp.sum(lax.all_gather(codeword_portion, "space"), axis=0)
     rendered = (
         images.reshape(tiles_here, 3, TILE_PIX)
         .transpose(1, 0, 2)

time: 952 us -> 786 us (0.83)
  waiting for transfers between devices: 495 us -> 325 us
    psum x1 -> x0, waiting for transfers between devices: 332 us -> none  [on_device(): code_grad = lax.psum(codeword_portion, 'space')]
    all_gather x0 -> x1, waiting for transfers between devices: none -> 171 us  [on_device(): code_grad = jnp.sum(lax.all_gather(codeword_portion, 'space'), axis=0)]
    reduce_sum x0 -> x1, other arithmetic: none -> 9.86 us  [on_device(): code_grad = jnp.sum(lax.all_gather(codeword_portion, 'space'), axis=0)]
  transfers between devices with their start and end apart: 5 -> 5, of which waited for: 4 -> 4; matrix products, arithmetic and copies ran while one was open for 4% -> 6% of each run, Pallas kernels for 0% -> 0%
where the time goes in v1:
time: 786 us; the launch traced here: 785 us
  waiting for transfers between devices  325 us (41%)
  blocking collectives  187 us (24%)
  other arithmetic  117 us (15%)
  local copies, waits for them, and re-layouts  64.4 us (8%)
  matrix products  39.7 us (5%)
  starting transfers between devices  35.9 us (5%)
  between operations  14.2 us (2%)
    all_to_all x1, blocking collectives, on_device(): lax.all_to_all(slot_grads, 'space', split_axis=1, concat_axis=1, tiled=True)  172 us
    all_gather x1, waiting for transfers between devices, on_device(): code_grad = jnp.sum(lax.all_gather(codeword_portion, 'space'), axis=0)  171 us
    all_to_all x1, waiting for transfers between devices, on_device(): lax.all_to_all(palette_out, 'space', split_axis=1, concat_axis=1, tiled=T...  71.7 us
    psum x1, waiting for transfers between devices, on_device(): resid_grad = lax.psum(resid_part, 'code')  47.8 us
    scatter-add x1, other arithmetic, on_device(): jax.ops.segment_sum(palette_owned.T, word_ids, num_segments=WORDS)  45.7 us
    reduce_scatter x1, waiting for transfers between devices, on_device(): lax.psum_scatter(word_term, 'code', scatter_dimension=1, tiled=True)  35.1 us
    dot_general x12, matrix products, composite(): mixed = jnp.dot(weight, palette.T, precision=lax.Precision.HIGHEST)  33.9 us
    another operation x21, other arithmetic  25.8 us
  transfers between devices with their start and end apart: 5, of which 4 were waited for; matrix products, arithmetic and copies ran while one was open for 6% of the time, Pallas kernels for 0%

profile of v1, /device:TPU:8, one launch (start us, length us, event | category | flops | bytes accessed | tf_op | source)
XLA Modules:
  0.0 784.8 jit_solution(4442039401856066829)
XLA Ops:
  7.2 0.7 compare_and_fusion.1
  8.5 0.7 gather_fusion
  9.2 0.9 select_bitcast_fusion.3
  10.2 19.5 %all-to-all-start = ((bf16[6,128,128]{2,0,1:T(8,128)(2,1)}), bf16[6,128,128]{2,0,1:T(8,128)(2,1)S(1)}, u32[]{:S(2)}, u32[]{:S(2)}) async-start(bf16[6,128,128]{2,0,1:T(8,128)(2,1)} %select_bitcast_fusion.3), calls=%async_computation | async-start | bytes 524288 | tf_op jit(solution)/shard_map/all_to_all | solution.py:121
  29.7 0.8 compare_and_fusion
  30.4 0.8 fusion.63
  31.2 1.1 copy.229
  32.3 14.9 %all_gather.9 = bf16[48,4096]{0,1:T(8,128)(2,1)S(1)} all-gather(bf16[48,1024]{0,1:T(8,128)(2,1)S(1)} %copy.229), channel_id=1, replica_groups=mesh['space'=128,'code'=4] {'code'}, dimensions={1}, use_global_device_ids=true | all-gather | bytes 491520 | tf_op jit(solution)/shard_map/all_gather | solution.py:115
  47.2 24.0 %gather_fusion.2 = bf16[8192,48]{1,0:T(8,128)(2,1)S(1)} fusion(bf16[48,4096]{0,1:T(8,128)(2,1)S(1)} %all_gather.9, s32[8192]{0:T(1024)S(1)} %fusion.63), kind=kCustom, calls=%fused_computation.2 | custom fusion | bytes 1605632 | tf_op jit(solution)/shard_map/jit(_take)/gather | solution.py:104
  71.2 0.8 copy.230
  73.4 0.9 gather_fusion.3
  74.3 1.4 select_bitcast_fusion
  75.7 16.2 %all-to-all-start.1 = ((bf16[48,128,128]{2,0,1:T(8,128)(2,1)}), bf16[48,128,128]{2,0,1:T(8,128)(2,1)S(1)}, u32[]{:S(2)}, u32[]{:S(2)}) async-start(bf16[48,128,128]{2,0,1:T(8,128)(2,1)} %select_bitcast_fusion), calls=%async_computation.1 | async-start | bytes 3145728 | tf_op jit(solution)/shard_map/all_to_all | solution.py:122
  93.6 1.5 gather_fusion.1
  95.2 71.7 %all-to-all-done.1 = bf16[48,128,128]{2,0,1:T(8,128)(2,1)S(1)} async-done(((bf16[48,128,128]{2,0,1:T(8,128)(2,1)}), bf16[48,128,128]{2,0,1:T(8,128)(2,1)S(1)}, u32[]{:S(2)}, u32[]{:S(2)}) %all-to-all-start.1) | async-done | bytes 1572896 | tf_op jit(solution)/shard_map/all_to_all | solution.py:122
  168.0 0.9 copy.255
  168.9 107.4 %while.16 = (s32[]{:T(128)}, f32[4,2,3,256]{3,1,0,2:T(2,128)}, f32[4,2,6,512]{3,2,1,0:T(8,128)S(1)}, f32[4,2,48,512]{3,2,1,0:T(8,128)}, bf16[4,2,6,512]{3,1,0,2:...) while((s32[]{:T(128)}, f32[4,2,3,256]{3,1,0,2:T(2,128)}, ...), condition=%wide.region_14.15_spmd.clone.clone, body=%wide.region_1.14_spmd.clone.clone.sunk | while | flops 552732160 | bytes 30296212 | solution.py:152
  169.9 1.9 fusion.93
  171.9 2.6 multiply_reduce_fusion.7
  175.5 2.6 fusion.94
  178.2 0.7 fusion.95
  179.5 2.4 fusion.98
  182.0 3.5 multiply_multiply_fusion.3
  186.4 4.3 fusion.96
  192.0 3.5 fusion.97
  196.7 1.9 fusion.93
  198.7 2.6 multiply_reduce_fusion.7
  202.3 2.5 fusion.94
  205.0 0.7 fusion.95
  206.3 2.4 fusion.98
  208.8 3.5 multiply_multiply_fusion.3
  213.2 4.3 fusion.96
  218.8 3.5 fusion.97
  223.5 1.9 fusion.93
  225.4 2.6 multiply_reduce_fusion.7
  229.1 2.6 fusion.94
  231.8 0.7 fusion.95
  233.1 2.4 fusion.98
  235.6 3.5 multiply_multiply_fusion.3
  240.0 4.3 fusion.96
  245.6 3.5 fusion.97
  250.3 1.9 fusion.93
  252.2 2.6 multiply_reduce_fusion.7
  255.8 2.6 fusion.94
  258.6 0.7 fusion.95
  259.9 2.5 fusion.98
  262.4 3.5 multiply_multiply_fusion.3
  266.8 4.3 fusion.96
  272.4 3.5 fusion.97
  276.2 2.3 concatenate.15
  279.2 4.1 convolution_bitcast_fusion.1
  283.3 3.2 copy.242
  286.5 171.7 %all_to_all.15 = f32[54,128,128]{2,0,1:T(8,128)S(1)} all-to-all(f32[54,128,128]{2,0,1:T(8,128)} %copy.242), channel_id=1, replica_groups=mesh['space'=128,'code'=4] {'space'}, dimensions={1} | all-to-all | bytes 7077888 | tf_op jit(solution)/shard_map/all_to_all | solution.py:176
  458.2 1.7 fusion.53
  460.1 2.7 copy.257
  462.8 45.7 %scatter_custom_fusion = f32[4096,48]{1,0:T(8,128)} fusion(s32[8192]{0:T(1024)} %param.12, f32[8192,48]{1,0:T(8,128)} %bitcast.187, f32[]{:T(128)} %constant.114.clone.1), kind=kCustom, calls=%fused_computation.109 | custom fusion | flops 393216 | bytes 786944 | tf_op jit(solution)/shard_map/scatter-add | solution.py:181
  508.5 35.1 %reduce-scatter.2.cloned.1.call-done = f32[48,1024]{0,1:T(8,128)} async-done(((f32[48,4096]{0,1:T(8,128)}), f32[48,1024]{0,1:T(8,128)}) %reduce-scatter.2.cloned.1.call-update) | async-done | bytes 196624 | tf_op jit(solution)/shard_map/reduce_scatter | solution.py:185
  543.6 1.9 copy.245
  545.7 1.1 copy.268
  547.5 0.7 slice.122
  548.2 170.6 %all-gather.3.cloned.1.call-done = f32[6144,1024]{1,0:T(8,128)} async-done(((f32[48,1024]{1,0:T(8,128)}), f32[6144,1024]{1,0:T(8,128)}) %all-gather.3.cloned.1.call-update) | async-done | bytes 25165840 | tf_op jit(solution)/shard_map/all_gather | solution.py:186
  718.7 9.9 %reduce_sum.90 = f32[48,1024]{1,0:T(8,128)} reduce(f32[128,48,1024]{2,1,0:T(8,128)} %bitcast.182, f32[]{:T(128)} %constant.114.clone.1), dimensions={0}, to_apply=%region_18.19 | reduce | flops 6242304 | bytes 25362436 | tf_op jit(solution)/shard_map/reduce_sum | solution.py:186
  728.6 47.8 %all-reduce.8.cloned.1.call-done = f32[12,8192]{1,0:T(8,128)} async-done(((f32[12,8192]{1,0:T(8,128)}), f32[12,8192]{1,0:T(8,128)}) %all-reduce.8.cloned.1.call-update) | async-done | bytes 393232 | tf_op jit(solution)/shard_map/psum | solution.py:184
  776.4 1.9 copy.343
  (268 shorter events, 26.5 us)
Async XLA Ops:
  7.2 1.4 copy-start
  10.2 65.5 %all-to-all-start = ((bf16[6,128,128]{2,0,1:T(8,128)(2,1)}), bf16[6,128,128]{2,0,1:T(8,128)(2,1)S(1)}, u32[]{:S(2)}, u32[]{:S(2)}) async-start(bf16[6,128,128]{2,0,1:T(8,128)(2,1)} %select_bitcast_fusion.3), calls=%async_computation | async-start | bytes 524288 | tf_op jit(solution)/shard_map/all_to_all | solution.py:121
  72.0 1.0 copy-start.3
  75.6 16.4 %copy-start.7 = (s32[1,8,4]{1,2,0:T(4,128)S(1)}, s32[1,8,4]{1,2,0:T(4,128)}, u32[]{:S(2)}) copy-start(s32[1,8,4]{1,2,0:T(4,128)} %param.15) | copy-start | bytes 388
  75.7 16.6 %copy-start.4 = (f32[1,3,2048]{2,0,1:T(1,128)S(1)}, f32[1,3,2048]{2,0,1:T(1,128)}, u32[]{:S(2)}) copy-start(f32[1,3,2048]{2,0,1:T(1,128)} %param.16) | copy-start | bytes 73732
  75.7 16.8 %copy-start.5 = (s32[1,3,2048]{2,0,1:T(1,128)S(1)}, s32[1,3,2048]{2,0,1:T(1,128)}, u32[]{:S(2)}) copy-start(s32[1,3,2048]{2,0,1:T(1,128)} %param.17) | copy-start | bytes 73732
  75.7 17.7 %copy-start.2 = (bf16[6,128,128]{2,0,1:T(8,128)(2,1)}, bf16[6,128,128]{2,0,1:T(8,128)(2,1)S(1)}, u32[]{:S(2)}) copy-start(bf16[6,128,128]{2,0,1:T(8,128)(2,1)S(1)} %all-to-all-done) | copy-start | bytes 589828
  75.7 91.3 %all-to-all-start.1 = ((bf16[48,128,128]{2,0,1:T(8,128)(2,1)}), bf16[48,128,128]{2,0,1:T(8,128)(2,1)S(1)}, u32[]{:S(2)}, u32[]{:S(2)}) async-start(bf16[48,128,128]{2,0,1:T(8,128)(2,1)} %select_bitcast_fusion), calls=%async_computation.1 | async-start | bytes 3145728 | tf_op jit(solution)/shard_map/all_to_all | solution.py:122
  91.9 451.7 %reduce-scatter.2.cloned.1.call-start = ((), (), s32[]{:S(2)}) async-start(), calls=%async_computation.5 | async-start | bytes 2621440 | tf_op jit(solution)/shard_map/reduce_scatter | solution.py:185
  286.5 171.7 %copy-start.8 = (s32[1,1,128]{2,1,0:T(1,128)S(1)}, s32[1,1,128]{2,1,0:T(1,128)}, u32[]{:S(2)}) copy-start(s32[1,1,128]{2,1,0:T(1,128)} %param.14) | copy-start | bytes 1540
  508.5 38.3 %copy-start.6 = (f32[4,2,3,256]{3,1,0,2:T(2,128)S(1)}, f32[4,2,3,256]{3,1,0,2:T(2,128)}, u32[]{:S(2)}) copy-start(f32[4,2,3,256]{3,1,0,2:T(2,128)} %get-tuple-element.64) | copy-start | bytes 73732
  508.5 210.2 %all-gather.3.cloned.1.call-start = ((), (), s32[]{:S(2)}) async-start(), calls=%async_computation.6 | async-start | bytes 25362432 | tf_op jit(solution)/shard_map/all_gather | solution.py:186
  545.5 230.9 %all-reduce.8.cloned.1.call-start = ((), (), s32[]{:S(2)}) async-start(), calls=%async_computation.4 | async-start | bytes 1048576 | tf_op jit(solution)/shard_map/psum | solution.py:184
  718.7 59.5 %copy-start.1 = (bf16[1,6,8192]{2,1,0:T(8,128)(2,1)S(1)}, bf16[1,6,8192]{2,1,0:T(8,128)(2,1)}, u32[]{:S(2)}) copy-start(bf16[1,6,8192]{2,1,0:T(8,128)(2,1)} %param.10) | copy-start | bytes 294916
Sparse Core Ops, SparseCore 0:
  508.6 34.9 reduce-scatter.1
  547.8 170.8 all-gather.2
  721.8 54.5 all-reduce.7
